TPU v7x, 256 devices: a whole 4x4x8 slice. The times are simulated.
256 devices in a mesh: group: 2 (over y_lo), branch: 16 (over y_hi, x, core), tensor: 8 (over z).
Axes of the slice: x: 4, y: 4 (y_hi: 2, y_lo: 2; y = y_hi * 2 + y_lo), z: 8, core: 2. Of those that a mesh axis runs over, the one named last changes fastest.
Arguments:
- queries: bfloat16 [8192, 8192], P(('group', 'branch'), 'tensor'), parts along dimension 0, may hold values from -160 to 160
- prefix_cache: bfloat16 [2, 3072, 1024], P(None, 'group', 'tensor'), parts along dimension 1, may hold values from -5 to 5
- prior_cache: bfloat16 [2, 8192, 1024], P(None, ('group', 'branch'), 'tensor'), parts along dimension 1, may hold values from -5 to 5
- fresh_cache: bfloat16 [2, 8192, 1024], P(None, ('group', 'branch'), 'tensor'), parts along dimension 1, may hold values from -5 to 5
- visible: int32 [32, 16], P('group'), parts along dimension 0, may hold values 0 or 1
- turn_order: int32 [32], P('group'), parts along dimension 0, may hold values from 0 to 15, each once
- output_weight: bfloat16 [8192, 8192], P('tensor', 'branch'), may hold values from -0.0625 to 0.0625
Outputs:
- projected: bfloat16 [8192, 8192], P(('group', 'branch'), 'tensor'), parts along dimension 0
There are 2 independent parts, one for each index of `group`. A program takes and returns all parts, laid end to end along the dimension named above; an argument that names none is the same for every part. Nothing has to cross between parts.
Inputs may be any that keep to these rules, and one draw needn't show every extreme that they name: `turn_order`: each of 0 to 15 once.
All inputs are finite; a program needn't handle non-finite values.
Results may differ from a plain program's by a relative error of at most 0.015.
Values may be sent and summed in bfloat16 or wider, within the bound.
A program may use at most 64 MiB of HBM per device.

v0:
```python
import math
import jax
import jax.numpy as jnp
from jax import lax
from jax.sharding import PartitionSpec as P

HD = 128
NEGATIVE = -1e30


def largest_divisor(total_rows, ceiling):
    chosen = 1
    for candidate in range(1, min(total_rows, ceiling) + 1):
        if total_rows % candidate == 0:
            chosen = candidate
    return chosen


def update_state(running, query_heads, key_rows, value_rows, allowed):
    peak_old, total_old, summed_old = running
    scores = jnp.einsum(
        "qhgd,khd->hgqk", query_heads, key_rows, preferred_element_type=jnp.float32
    ) / math.sqrt(HD)
    if allowed is None:
        masked = scores
    else:
        masked = jnp.where(allowed, scores, NEGATIVE)
    peak_new = jnp.maximum(peak_old, jnp.max(masked, axis=-1))
    weights = jnp.exp(masked - peak_new[..., None])
    if allowed is not None:
        weights = jnp.where(allowed, weights, 0.0)
    factor = jnp.exp(peak_old - peak_new)
    total_new = total_old * factor + jnp.sum(weights, axis=-1)
    summed_new = summed_old * factor[..., None] + jnp.einsum(
        "hgqk,khd->hgqd",
        weights.astype(jnp.bfloat16),
        value_rows,
        preferred_element_type=jnp.float32,
    )
    return (peak_new, total_new, summed_new)


def sweep(running, query_heads, key_rows, value_rows, allow_rows):
    row_count = key_rows.shape[0]
    block_rows = largest_divisor(row_count, 1024)
    if block_rows == row_count:
        return update_state(running, query_heads, key_rows, value_rows, allow_rows(0, row_count))
    block_count = row_count // block_rows
    key_blocks = key_rows.reshape(block_count, block_rows, key_rows.shape[1], key_rows.shape[2])
    value_blocks = value_rows.reshape(
        block_count, block_rows, value_rows.shape[1], value_rows.shape[2]
    )

    def advance(state, inputs):
        key_block, value_block, position = inputs
        return (
            update_state(
                state,
                query_heads,
                key_block,
                value_block,
                allow_rows(position * block_rows, block_rows),
            ),
            None,
        )

    running, unused = lax.scan(
        advance, running, (key_blocks, value_blocks, jnp.arange(block_count, dtype=jnp.int32))
    )
    return running


def per_device(queries, prefix_cache, prior_cache, fresh_cache, visible, turn_order, output_weight):
    message_rows = queries.shape[0]
    local_heads = queries.shape[1] // HD
    local_groups = prefix_cache.shape[2] // HD
    sharing = local_heads // local_groups
    query_heads = queries.reshape(message_rows, local_groups, sharing, HD)
    agent_index = lax.axis_index("branch")
    agent_count = visible.shape[0]
    seen_row = lax.dynamic_slice_in_dim(visible, agent_index, 1, 0)[0]
    own_turn = lax.dynamic_slice_in_dim(turn_order, agent_index, 1, 0)[0]
    positions = jnp.arange(message_rows, dtype=jnp.int32)
    agent_ids = jnp.arange(agent_count, dtype=jnp.int32)

    def split_cache(cache):
        return (cache[0].reshape(-1, local_groups, HD), cache[1].reshape(-1, local_groups, HD))

    def whole_rows(offset, count):
        return None

    start_state = (
        jnp.full((local_groups, sharing, message_rows), NEGATIVE, jnp.float32),
        jnp.zeros((local_groups, sharing, message_rows), jnp.float32),
        jnp.zeros((local_groups, sharing, message_rows, HD), jnp.float32),
    )
    prefix_keys, prefix_values = split_cache(prefix_cache)
    prefix_state = sweep(start_state, query_heads, prefix_keys, prefix_values, whole_rows)

    def add_messages(running, pieces, root):
        prior_keys, prior_values = split_cache(pieces[0])
        fresh_keys, fresh_values = split_cache(pieces[1])

        def locate(offset, count):
            row_index = root + offset + jnp.arange(count, dtype=jnp.int32)
            owner_ids = row_index // message_rows
            onehot = owner_ids[:, None] == agent_ids[None, :]
            return (row_index, owner_ids, onehot)

        def prior_allowed(offset, count):
            row_index, owner_ids, onehot = locate(offset, count)
            visible_rows = jnp.sum(jnp.where(onehot, seen_row[None, :], 0), axis=1) > 0
            return visible_rows[None, :]

        def fresh_allowed(offset, count):
            row_index, owner_ids, onehot = locate(offset, count)
            turn_values = jnp.sum(jnp.where(onehot, turn_order[None, :], 0), axis=1)
            earlier = turn_values < own_turn
            causal = (owner_ids == agent_index)[None, :] & (
                (row_index % message_rows)[None, :] <= positions[:, None]
            )
            return earlier[None, :] | causal

        running = sweep(running, query_heads, prior_keys, prior_values, prior_allowed)
        return sweep(running, query_heads, fresh_keys, fresh_values, fresh_allowed)

    peak_final, total_final, summed_final = add_messages(
        prefix_state,
        (
            lax.all_gather(prior_cache, "branch", axis=1, tiled=True),
            lax.all_gather(fresh_cache, "branch", axis=1, tiled=True),
        ),
        jnp.int32(0),
    )
    heads_out = (summed_final / total_final[..., None]).astype(jnp.bfloat16)
    attention = jnp.transpose(heads_out, (2, 0, 1, 3)).reshape(message_rows, local_heads * HD)
    product = jnp.dot(
        lax.all_gather(attention, "branch", axis=0, tiled=True),
        output_weight,
        preferred_element_type=jnp.float32,
    )
    partial_columns = product.astype(jnp.bfloat16).astype(jnp.float32)
    column_totals = lax.psum_scatter(
        partial_columns.astype(jnp.bfloat16), "tensor", scatter_dimension=1, tiled=True
    )
    result = lax.all_to_all(column_totals, "branch", split_axis=0, concat_axis=1, tiled=True)
    return result


def solution(mesh):
    return jax.shard_map(
        per_device,
        mesh=mesh,
        in_specs=(
            P(("group", "branch"), "tensor"),
            P(None, "group", "tensor"),
            P(None, ("group", "branch"), "tensor"),
            P(None, ("group", "branch"), "tensor"),
            P("group", None),
            P("group"),
            P("tensor", "branch"),
        ),
        out_specs=P(("group", "branch"), "tensor"),
        check_vma=False,
    )
```

profile of v0, /device:TPU:1, one launch (start us, length us, event | category | flops | bytes accessed | tf_op | source)
XLA Modules:
  0.0 348.3 jit_solution(16154351550768117709)
XLA Ops:
  8.1 1.2 copy.25
  9.6 1.2 fusion.94
  10.8 18.8 %while.51 = (s32[]{:T(128)}, f32[1,8,256]{2,1,0:T(8,128)S(1)}, f32[1,8,256]{2,1,0:T(8,128)S(1)}, f32[1,8,256,128]{3,2,1,0:T(8,128)S(1)}, bf16[2,768,1,128]{3,1,2...) while((s32[]{:T(128)}, f32[1,8,256]{2,1,0:T(8,128)S(1)}, ...), condition=%wide.region_3.4_spmd.clone, body=%wide.region_0.3_spmd.clone.sunk | while | flops 818688000 | bytes 47186060 | solution.py:67
  10.8 3.6 %bitcast_reduce_fusion.5 = (f32[8,256]{1,0:T(8,128)S(1)}, f32[768,256,8]{1,0,2:T(8,128)}) fusion(bf16[256,1,8,128]{3,0,2,1:T(8,128)(2,1)S(1)} %get-tuple-element.758, bf16[2,768,1,128]{3,1,2,0:T(8,128)(2,1)S(1)} %get-tuple-element.757, s32[]{:T(128)} %get-tuple-element.744), kind=kOutput, calls=%fused_computation.88.clone.1 | convolution fusion | flops 405796864 | bytes 7020548 | tf_op jit(solution)/shard_map/while/body/eval_jaxpr/qhgd,khd->hgqk/dot_general | solution.py:21
  14.5 4.5 %fusion.130 = f32[1,8,256,128]{3,2,1,0:T(8,128)S(1)} fusion(f32[768,256,8]{1,0,2:T(8,128)} %get-tuple-element.733, f32[8,256]{1,0:T(8,128)S(1)} %bitcast.284, f32[1,8,256,128]{3,2,1,0:T(8,128)S(1)} %get-tuple-element.747, f32[8,256]{1,0:T(8,128)S(1)} %get-tuple-element.734, pred[]{:T(512)S(6)} %compare.35, ...), kind=kOutput, calls=%fused_computation.97.clone.1 | convolution fusion | flops 408158208 | bytes 8601605 | tf_op jit(solution)/shard_map/while/body/eval_jaxpr/hgqk,khd->hgqd/dot_general | solution.py:34
  19.0 1.1 fusion.129
  20.1 3.6 %bitcast_reduce_fusion.5 = (f32[8,256]{1,0:T(8,128)S(1)}, f32[768,256,8]{1,0,2:T(8,128)}) fusion(bf16[256,1,8,128]{3,0,2,1:T(8,128)(2,1)S(1)} %get-tuple-element.758, bf16[2,768,1,128]{3,1,2,0:T(8,128)(2,1)S(1)} %get-tuple-element.757, s32[]{:T(128)} %get-tuple-element.744), kind=kOutput, calls=%fused_computation.88.clone.1 | convolution fusion | flops 405796864 | bytes 7020548 | tf_op jit(solution)/shard_map/while/body/eval_jaxpr/qhgd,khd->hgqk/dot_general | solution.py:21
  23.8 4.6 %fusion.130 = f32[1,8,256,128]{3,2,1,0:T(8,128)S(1)} fusion(f32[768,256,8]{1,0,2:T(8,128)} %get-tuple-element.733, f32[8,256]{1,0:T(8,128)S(1)} %bitcast.284, f32[1,8,256,128]{3,2,1,0:T(8,128)S(1)} %get-tuple-element.747, f32[8,256]{1,0:T(8,128)S(1)} %get-tuple-element.734, pred[]{:T(512)S(6)} %compare.35, ...), kind=kOutput, calls=%fused_computation.97.clone.1 | convolution fusion | flops 408158208 | bytes 8601605 | tf_op jit(solution)/shard_map/while/body/eval_jaxpr/hgqk,khd->hgqd/dot_general | solution.py:34
  28.5 1.1 fusion.129
  30.9 37.0 %all-gather.4.cloned.1.call-done = bf16[2,4096,128]{2,1,0:T(8,128)(2,1)} async-done(((bf16[2,256,128]{2,1,0:T(8,128)(2,1)}), bf16[2,4096,128]{2,1,0:T(8,128)(2,1)}) %all-gather.4.cloned.1.call-update) | async-done | bytes 2097168 | tf_op jit(solution)/shard_map/all_gather | solution.py:130
  67.9 3.0 fusion.93
  70.9 42.6 %while.49 = (s32[]{:T(128)}, f32[1,8,256]{2,1,0:T(8,128)S(1)}, f32[1,8,256]{2,1,0:T(8,128)S(1)}, f32[1,8,256,128]{3,2,1,0:T(8,128)S(1)}, s32[4]{0:T(128)S(1)}, /...) while((s32[]{:T(128)}, f32[1,8,256]{2,1,0:T(8,128)S(1)}, ...), condition=%wide.region_8.9_spmd.clone, body=%wide.region_4.8_spmd.clone.sunk | while | flops 1101600768 | bytes 28465352 | solution.py:67
  72.2 2.5 bitcast_reduce_fusion.4
  74.8 4.2 %fusion.118 = f32[1,8,256,128]{3,2,1,0:T(8,128)S(1)} fusion(f32[1024,256,8]{1,0,2:T(8,128)S(1)} %get-tuple-element.705, f32[8,256]{1,0:T(8,128)S(1)} %bitcast.288, pred[1024]{0:T(1024)(128)(4,1)S(1)} %broadcast_compare_fusion.5, f32[1,8,256,128]{3,2,1,0:T(8,128)S(1)} %get-tuple-element.776, f32[8,256]{1,0:T(8,128)S(1)} %get-tuple-element.706, ...), kind=kOutput, calls=%fused_computation.15.clone.1 | convolution fusion | flops 547880960 | bytes 10766848 | tf_op jit(solution)/shard_map/while/body/eval_jaxpr/hgqk,khd->hgqd/dot_general | solution.py:34
  78.9 2.6 fusion.117
  82.8 2.5 bitcast_reduce_fusion.4
  85.4 4.2 %fusion.118 = f32[1,8,256,128]{3,2,1,0:T(8,128)S(1)} fusion(f32[1024,256,8]{1,0,2:T(8,128)S(1)} %get-tuple-element.705, f32[8,256]{1,0:T(8,128)S(1)} %bitcast.288, pred[1024]{0:T(1024)(128)(4,1)S(1)} %broadcast_compare_fusion.5, f32[1,8,256,128]{3,2,1,0:T(8,128)S(1)} %get-tuple-element.776, f32[8,256]{1,0:T(8,128)S(1)} %get-tuple-element.706, ...), kind=kOutput, calls=%fused_computation.15.clone.1 | convolution fusion | flops 547880960 | bytes 10766848 | tf_op jit(solution)/shard_map/while/body/eval_jaxpr/hgqk,khd->hgqd/dot_general | solution.py:34
  89.6 2.6 fusion.117
  93.5 2.5 bitcast_reduce_fusion.4
  96.0 4.2 %fusion.118 = f32[1,8,256,128]{3,2,1,0:T(8,128)S(1)} fusion(f32[1024,256,8]{1,0,2:T(8,128)S(1)} %get-tuple-element.705, f32[8,256]{1,0:T(8,128)S(1)} %bitcast.288, pred[1024]{0:T(1024)(128)(4,1)S(1)} %broadcast_compare_fusion.5, f32[1,8,256,128]{3,2,1,0:T(8,128)S(1)} %get-tuple-element.776, f32[8,256]{1,0:T(8,128)S(1)} %get-tuple-element.706, ...), kind=kOutput, calls=%fused_computation.15.clone.1 | convolution fusion | flops 547880960 | bytes 10766848 | tf_op jit(solution)/shard_map/while/body/eval_jaxpr/hgqk,khd->hgqd/dot_general | solution.py:34
  100.2 2.6 fusion.117
  104.1 2.6 bitcast_reduce_fusion.4
  106.7 4.2 %fusion.118 = f32[1,8,256,128]{3,2,1,0:T(8,128)S(1)} fusion(f32[1024,256,8]{1,0,2:T(8,128)S(1)} %get-tuple-element.705, f32[8,256]{1,0:T(8,128)S(1)} %bitcast.288, pred[1024]{0:T(1024)(128)(4,1)S(1)} %broadcast_compare_fusion.5, f32[1,8,256,128]{3,2,1,0:T(8,128)S(1)} %get-tuple-element.776, f32[8,256]{1,0:T(8,128)S(1)} %get-tuple-element.706, ...), kind=kOutput, calls=%fused_computation.15.clone.1 | convolution fusion | flops 547880960 | bytes 10766848 | tf_op jit(solution)/shard_map/while/body/eval_jaxpr/hgqk,khd->hgqd/dot_general | solution.py:34
  110.9 2.6 fusion.117
  113.5 9.6 %all-gather.6.cloned.1.call-done = bf16[2,4096,128]{2,1,0:T(8,128)(2,1)} async-done(((bf16[2,256,128]{2,1,0:T(8,128)(2,1)}), bf16[2,4096,128]{2,1,0:T(8,128)(2,1)}) %all-gather.6.cloned.1.call-update) | async-done | bytes 2097168 | tf_op jit(solution)/shard_map/all_gather | solution.py:131
  123.1 3.0 fusion.92
  126.1 44.2 %while.50 = (s32[]{:T(128)}, f32[1,8,256]{2,1,0:T(8,128)S(1)}, f32[1,8,256]{2,1,0:T(8,128)S(1)}, f32[1,8,256,128]{3,2,1,0:T(8,128)S(1)}, s32[4]{0:T(128)S(1)}, /...) while((s32[]{:T(128)}, f32[1,8,256]{2,1,0:T(8,128)S(1)}, ...), condition=%wide.region_13.14_spmd.clone, body=%wide.region_9.13_spmd.clone.sunk | while | flops 1102416896 | bytes 29521128 | solution.py:67
  128.0 1.0 fusion.121
  129.0 2.3 fusion.122
  131.4 3.7 %fusion.125 = f32[1,8,256,128]{3,2,1,0:T(8,128)S(1)} fusion(f32[1024,256,8]{1,0,2:T(8,128)S(1)} %get-tuple-element.722, f32[8,256]{1,0:T(8,128)S(1)} %bitcast.290, pred[256,1024]{0,1:T(8,128)(4,1)S(1)} %fusion.121, f32[1,8,256,128]{3,2,1,0:T(8,128)S(1)} %get-tuple-element.811, f32[8,256]{1,0:T(8,128)S(1)} %get-tuple-element.723, ...), kind=kOutput, calls=%fused_computation.52.clone.1 | convolution fusion | flops 547880960 | bytes 11026944 | tf_op jit(solution)/shard_map/while/body/eval_jaxpr/hgqk,khd->hgqd/dot_general | solution.py:34
  135.1 2.0 fusion.124
  140.1 2.3 fusion.122
  142.4 3.7 %fusion.125 = f32[1,8,256,128]{3,2,1,0:T(8,128)S(1)} fusion(f32[1024,256,8]{1,0,2:T(8,128)S(1)} %get-tuple-element.722, f32[8,256]{1,0:T(8,128)S(1)} %bitcast.290, pred[256,1024]{0,1:T(8,128)(4,1)S(1)} %fusion.121, f32[1,8,256,128]{3,2,1,0:T(8,128)S(1)} %get-tuple-element.811, f32[8,256]{1,0:T(8,128)S(1)} %get-tuple-element.723, ...), kind=kOutput, calls=%fused_computation.52.clone.1 | convolution fusion | flops 547880960 | bytes 11026944 | tf_op jit(solution)/shard_map/while/body/eval_jaxpr/hgqk,khd->hgqd/dot_general | solution.py:34
  146.1 2.0 fusion.124
  151.1 2.3 fusion.122
  153.5 3.7 %fusion.125 = f32[1,8,256,128]{3,2,1,0:T(8,128)S(1)} fusion(f32[1024,256,8]{1,0,2:T(8,128)S(1)} %get-tuple-element.722, f32[8,256]{1,0:T(8,128)S(1)} %bitcast.290, pred[256,1024]{0,1:T(8,128)(4,1)S(1)} %fusion.121, f32[1,8,256,128]{3,2,1,0:T(8,128)S(1)} %get-tuple-element.811, f32[8,256]{1,0:T(8,128)S(1)} %get-tuple-element.723, ...), kind=kOutput, calls=%fused_computation.52.clone.1 | convolution fusion | flops 547880960 | bytes 11026944 | tf_op jit(solution)/shard_map/while/body/eval_jaxpr/hgqk,khd->hgqd/dot_general | solution.py:34
  157.2 2.0 fusion.124
  162.2 2.3 fusion.122
  164.5 3.7 %fusion.125 = f32[1,8,256,128]{3,2,1,0:T(8,128)S(1)} fusion(f32[1024,256,8]{1,0,2:T(8,128)S(1)} %get-tuple-element.722, f32[8,256]{1,0:T(8,128)S(1)} %bitcast.290, pred[256,1024]{0,1:T(8,128)(4,1)S(1)} %fusion.121, f32[1,8,256,128]{3,2,1,0:T(8,128)S(1)} %get-tuple-element.811, f32[8,256]{1,0:T(8,128)S(1)} %get-tuple-element.723, ...), kind=kOutput, calls=%fused_computation.52.clone.1 | convolution fusion | flops 547880960 | bytes 11026944 | tf_op jit(solution)/shard_map/while/body/eval_jaxpr/hgqk,khd->hgqd/dot_general | solution.py:34
  168.3 2.0 fusion.124
  170.3 1.3 copy.29
  171.6 2.1 divide_convert_fusion
  173.8 84.2 %all-gather.8.cloned.1.call-done = bf16[4096,1024]{0,1:T(8,128)(2,1)} async-done(((bf16[256,1024]{0,1:T(8,128)(2,1)}), bf16[4096,1024]{0,1:T(8,128)(2,1)}) %all-gather.8.cloned.1.call-update) | async-done | bytes 8388624 | tf_op jit(solution)/shard_map/all_gather | solution.py:138
  258.0 9.5 %convolution_convert_fusion = bf16[4096,512]{0,1:T(8,128)(2,1)} fusion(bf16[4096,1024]{0,1:T(8,128)(2,1)} %all-gather.8.cloned.1.call-done, bf16[1024,512]{1,0:T(8,128)(2,1)S(1)} %copy-done), kind=kOutput, calls=%fused_computation.113 | convolution fusion | flops 4297064448 | bytes 13631488 | tf_op jit(solution)/shard_map/dot_general | solution.py:137
  267.6 53.6 %reduce-scatter.2.cloned.1.call-done = bf16[4096,64]{0,1:T(8,128)(2,1)} async-done(((bf16[4096,512]{0,1:T(8,128)(2,1)}), bf16[4096,64]{0,1:T(8,128)(2,1)}) %reduce-scatter.2.cloned.1.call-update) | async-done | bytes 524304 | tf_op jit(solution)/shard_map/reduce_scatter | solution.py:143
  321.2 1.1 copy.37
  322.3 18.5 %all_to_all.19 = bf16[16,256,64]{1,2,0:T(8,128)(2,1)S(1)} all-to-all(bf16[16,256,64]{1,2,0:T(8,128)(2,1)S(1)} %bitcast.294), channel_id=1, replica_groups=mesh['group'=2,'branch'=16,'tensor'=8] {'branch'}, dimensions={0} | all-to-all | bytes 1048576 | tf_op jit(solution)/shard_map/all_to_all | solution.py:146
  340.8 1.0 copy.31
  (93 shorter events, 14.4 us)
Async XLA Ops:
  6.5 251.5 %copy-start = (bf16[1024,512]{1,0:T(8,128)(2,1)S(1)}, bf16[1024,512]{1,0:T(8,128)(2,1)}, u32[]{:S(2)}) copy-start(bf16[1024,512]{1,0:T(8,128)(2,1)} %param.19) | copy-start | bytes 3145732
  6.5 61.3 %all-gather.4.cloned.1.call-start = ((), (), s32[]{:S(2)}) async-start(), calls=%async_computation.2 | async-start | bytes 2228224 | tf_op jit(solution)/shard_map/all_gather | solution.py:130
  7.3 115.8 %all-gather.6.cloned.1.call-start = ((), (), s32[]{:S(2)}) async-start(), calls=%async_computation.3 | async-start | bytes 2228224 | tf_op jit(solution)/shard_map/all_gather | solution.py:131
  8.0 250.0 %all-gather.8.cloned.1.call-start = ((), (), s32[]{:S(2)}) async-start(), calls=%async_computation.4 | async-start | bytes 8912896 | tf_op jit(solution)/shard_map/all_gather | solution.py:138
  10.8 19.5 %copy-start.2 = (s32[16]{0:T(128)S(1)}, s32[16]{0:T(128)}, u32[]{:S(2)}) copy-start(s32[16]{0:T(128)} %param.18) | copy-start | bytes 196
  14.4 4.6 %copy-start.1 = (f32[768,256,8]{1,0,2:T(8,128)S(1)}, f32[768,256,8]{1,0,2:T(8,128)}, u32[]{:S(2)}) copy-start(f32[768,256,8]{1,0,2:T(8,128)} %get-tuple-element.733) | copy-start | bytes 18874372 | tf_op jit(solution)/shard_map/while
  23.8 4.8 %copy-start.1 = (f32[768,256,8]{1,0,2:T(8,128)S(1)}, f32[768,256,8]{1,0,2:T(8,128)}, u32[]{:S(2)}) copy-start(f32[768,256,8]{1,0,2:T(8,128)} %get-tuple-element.733) | copy-start | bytes 18874372 | tf_op jit(solution)/shard_map/while
  173.8 147.4 %reduce-scatter.2.cloned.1.call-start = ((), (), s32[]{:S(2)}) async-start(), calls=%async_computation.5 | async-start | bytes 4718592 | tf_op jit(solution)/shard_map/reduce_scatter | solution.py:143
Sparse Core Ops, SparseCore 0:
  10.1 57.6 all-gather.3
  70.6 52.3 all-gather.5
  173.9 84.0 all-gather.7
  267.7 53.4 reduce-scatter.1
where the time goes:
time: 349 us; the launch traced here: 348 us
  waiting for transfers between devices  186 us (53%)
  matrix products  77 us (22%)
  other arithmetic  29.6 us (8%)
  local copies, waits for them, and re-layouts  18.5 us (5%)
  blocking collectives  18.5 us (5%)
  between operations  13.2 us (4%)
  loops' own time  5.53 us (2%)
    all_gather x1, waiting for transfers between devices, per_device(): lax.all_gather(attention, 'branch', axis=0, tiled=True)  84.2 us
    reduce_scatter x1, waiting for transfers between devices, per_device(): lax.psum_scatter(partial_columns.astype(jnp.bfloat16), 'tensor', scatter_...  53.6 us
    dot_general x10, matrix products, update_state(): jnp.einsum('hgqk,khd->hgqd', weights.astype(jnp.bfloat16), value_rows, pr...  40.6 us
    all_gather x1, waiting for transfers between devices, per_device(): lax.all_gather(prior_cache, 'branch', axis=1, tiled=True)  37 us
    dot_general x10, matrix products, update_state(): jnp.einsum('qhgd,khd->hgqk', query_heads, key_rows, preferred_element_typ...  26.9 us
    reduce_sum x10, other arithmetic, update_state(): total_new = total_old * factor + jnp.sum(weights, axis=-1)  20.4 us
    all_to_all x1, blocking collectives, per_device(): lax.all_to_all(column_totals, 'branch', split_axis=0, concat_axis=1, tile...  18.5 us
    all_gather x1, waiting for transfers between devices, per_device(): lax.all_gather(fresh_cache, 'branch', axis=1, tiled=True)  9.58 us
  transfers between devices with their start and end apart: 4, of which 4 were waited for; matrix products, arithmetic and copies ran while one was open for 19% of the time, Pallas kernels for 0%

commit v1 on v0

--- a/solution.py
+++ b/solution.py
@@ -127,7 +127,10 @@
     peak_final, total_final, summed_final = add_messages(
         prefix_state,
         (
-            lax.all_gather(prior_cache, "branch", axis=1, tiled=True),
+            jnp.concatenate(
+                lax.all_to_all(jnp.stack([prior_cache] * lax.axis_size("branch")), "branch", 0, 0),
+                axis=1,
+            ),
             lax.all_gather(fresh_cache, "branch", axis=1, tiled=True),
         ),
         jnp.int32(0),

time: 349 us -> 322 us (0.923)
  waiting for transfers between devices: 186 us -> 147 us
  starting transfers between devices: 0.12 us -> 8.56 us
    all_gather x1 -> x0, waiting for transfers between devices: 37 us -> none  [per_device(): lax.all_gather(prior_cache, 'branch', axis=1, tiled=True)]
    all_gather x1, waiting for transfers between devices: 9.58 us -> 0.02 us  [per_device(): lax.all_gather(fresh_cache, 'branch', axis=1, tiled=True)]
    all_to_all x0 -> x1, starting transfers between devices: none -> 8.45 us  [per_device(): lax.all_to_all(jnp.stack([prior_cache] * lax.axis_size('branch')), 'branc...]
    all_to_all x0 -> x1, waiting for transfers between devices: none -> 6.11 us  [per_device(): lax.all_to_all(jnp.stack([prior_cache] * lax.axis_size('branch')), 'branc...]
  transfers between devices with their start and end apart: 4 -> 4, of which waited for: 4 -> 3; matrix products, arithmetic and copies ran while one was open for 19% -> 20% of each run, Pallas kernels for 0% -> 0%
where the time goes in v1:
time: 322 us; the launch traced here: 321 us
  waiting for transfers between devices  147 us (46%)
  matrix products  77 us (24%)
  other arithmetic  29.9 us (9%)
  local copies, waits for them, and re-layouts  21.5 us (7%)
  blocking collectives  18.5 us (6%)
  between operations  13.2 us (4%)
  starting transfers between devices  8.56 us (3%)
  loops' own time  5.6 us (2%)
    all_gather x1, waiting for transfers between devices, per_device(): lax.all_gather(attention, 'branch', axis=0, tiled=True)  86.7 us
    reduce_scatter x1, waiting for transfers between devices, per_device(): lax.psum_scatter(partial_columns.astype(jnp.bfloat16), 'tensor', scatter_...  53.6 us
    dot_general x10, matrix products, update_state(): jnp.einsum('hgqk,khd->hgqd', weights.astype(jnp.bfloat16), value_rows, pr...  40.6 us
    dot_general x10, matrix products, update_state(): jnp.einsum('qhgd,khd->hgqk', query_heads, key_rows, preferred_element_typ...  26.9 us
    reduce_sum x10, other arithmetic, update_state(): total_new = total_old * factor + jnp.sum(weights, axis=-1)  20.4 us
    all_to_all x1, blocking collectives, per_device(): lax.all_to_all(column_totals, 'branch', split_axis=0, concat_axis=1, tile...  18.5 us
    dot_general x1, matrix products, per_device(): jnp.dot(lax.all_gather(attention, 'branch', axis=0, tiled=True), output_w...  9.55 us
    all_to_all x1, starting transfers between devices, per_device(): lax.all_to_all(jnp.stack([prior_cache] * lax.axis_size('branch')), 'branc...  8.45 us
  transfers between devices with their start and end apart: 4, of which 3 were waited for; matrix products, arithmetic and copies ran while one was open for 20% of the time, Pallas kernels for 0%

profile of v1, /device:TPU:1, one launch (start us, length us, event | category | flops | bytes accessed | tf_op | source)
XLA Modules:
  0.0 321.4 jit_solution(4752608446305261824)
XLA Ops:
  6.5 2.8 stack.2
  9.3 8.4 %all-to-all-start = ((bf16[16,2,256,128]{3,2,1,0:T(8,128)(2,1)}), bf16[16,2,256,128]{3,2,1,0:T(8,128)(2,1)}, u32[]{:S(2)}, u32[]{:S(2)}) async-start(bf16[16,2,256,128]{3,2,1,0:T(8,128)(2,1)} %stack.2), calls=%async_computation | async-start | bytes 4194304 | tf_op jit(solution)/shard_map/all_to_all | solution.py:131
  18.6 1.2 copy.37
  20.1 1.2 fusion.94
  22.6 18.8 %while.51 = (s32[]{:T(128)}, f32[1,8,256]{2,1,0:T(8,128)S(1)}, f32[1,8,256]{2,1,0:T(8,128)S(1)}, f32[1,8,256,128]{3,2,1,0:T(8,128)S(1)}, bf16[2,768,1,128]{3,1,2...) while((s32[]{:T(128)}, f32[1,8,256]{2,1,0:T(8,128)S(1)}, ...), condition=%wide.region_3.4_spmd.clone, body=%wide.region_0.3_spmd.clone.sunk | while | flops 818688000 | bytes 47186060 | solution.py:67
  22.6 3.6 %bitcast_reduce_fusion.5 = (f32[8,256]{1,0:T(8,128)S(1)}, f32[768,256,8]{1,0,2:T(8,128)}) fusion(bf16[256,1,8,128]{3,0,2,1:T(8,128)(2,1)S(1)} %get-tuple-element.785, bf16[2,768,1,128]{3,1,2,0:T(8,128)(2,1)S(1)} %get-tuple-element.784, s32[]{:T(128)} %get-tuple-element.771), kind=kOutput, calls=%fused_computation.88.clone.1 | convolution fusion | flops 405796864 | bytes 7020548 | tf_op jit(solution)/shard_map/while/body/eval_jaxpr/qhgd,khd->hgqk/dot_general | solution.py:21
  26.3 4.5 %fusion.130 = f32[1,8,256,128]{3,2,1,0:T(8,128)S(1)} fusion(f32[768,256,8]{1,0,2:T(8,128)} %get-tuple-element.760, f32[8,256]{1,0:T(8,128)S(1)} %bitcast.289, f32[1,8,256,128]{3,2,1,0:T(8,128)S(1)} %get-tuple-element.774, f32[8,256]{1,0:T(8,128)S(1)} %get-tuple-element.761, pred[]{:T(512)S(6)} %compare.35, ...), kind=kOutput, calls=%fused_computation.97.clone.1 | convolution fusion | flops 408158208 | bytes 8601605 | tf_op jit(solution)/shard_map/while/body/eval_jaxpr/hgqk,khd->hgqd/dot_general | solution.py:34
  30.9 1.1 fusion.129
  32.0 3.6 %bitcast_reduce_fusion.5 = (f32[8,256]{1,0:T(8,128)S(1)}, f32[768,256,8]{1,0,2:T(8,128)}) fusion(bf16[256,1,8,128]{3,0,2,1:T(8,128)(2,1)S(1)} %get-tuple-element.785, bf16[2,768,1,128]{3,1,2,0:T(8,128)(2,1)S(1)} %get-tuple-element.784, s32[]{:T(128)} %get-tuple-element.771), kind=kOutput, calls=%fused_computation.88.clone.1 | convolution fusion | flops 405796864 | bytes 7020548 | tf_op jit(solution)/shard_map/while/body/eval_jaxpr/qhgd,khd->hgqk/dot_general | solution.py:21
  35.6 4.6 %fusion.130 = f32[1,8,256,128]{3,2,1,0:T(8,128)S(1)} fusion(f32[768,256,8]{1,0,2:T(8,128)} %get-tuple-element.760, f32[8,256]{1,0:T(8,128)S(1)} %bitcast.289, f32[1,8,256,128]{3,2,1,0:T(8,128)S(1)} %get-tuple-element.774, f32[8,256]{1,0:T(8,128)S(1)} %get-tuple-element.761, pred[]{:T(512)S(6)} %compare.35, ...), kind=kOutput, calls=%fused_computation.97.clone.1 | convolution fusion | flops 408158208 | bytes 8601605 | tf_op jit(solution)/shard_map/while/body/eval_jaxpr/hgqk,khd->hgqd/dot_general | solution.py:34
  40.3 1.1 fusion.129
  41.4 6.1 %all-to-all-done = bf16[16,2,256,128]{3,2,1,0:T(8,128)(2,1)} async-done(((bf16[16,2,256,128]{3,2,1,0:T(8,128)(2,1)}), bf16[16,2,256,128]{3,2,1,0:T(8,128)(2,1)}, u32[]{:S(2)}, u32[]{:S(2)}) %all-to-all-start) | async-done | bytes 2097184 | tf_op jit(solution)/shard_map/all_to_all | solution.py:131
  47.5 3.1 fusion.93
  50.7 42.8 %while.49 = (s32[]{:T(128)}, f32[1,8,256]{2,1,0:T(8,128)S(1)}, f32[1,8,256]{2,1,0:T(8,128)S(1)}, f32[1,8,256,128]{3,2,1,0:T(8,128)S(1)}, s32[4]{0:T(128)S(1)}, /...) while((s32[]{:T(128)}, f32[1,8,256]{2,1,0:T(8,128)S(1)}, ...), condition=%wide.region_8.9_spmd.clone, body=%wide.region_4.8_spmd.clone.sunk | while | flops 1101600768 | bytes 28465352 | solution.py:67
  52.0 2.6 bitcast_reduce_fusion.4
  54.6 4.2 %fusion.118 = f32[1,8,256,128]{3,2,1,0:T(8,128)S(1)} fusion(f32[1024,256,8]{1,0,2:T(8,128)S(1)} %get-tuple-element.732, f32[8,256]{1,0:T(8,128)S(1)} %bitcast.293, pred[1024]{0:T(1024)(128)(4,1)S(1)} %broadcast_compare_fusion.5, f32[1,8,256,128]{3,2,1,0:T(8,128)S(1)} %get-tuple-element.803, f32[8,256]{1,0:T(8,128)S(1)} %get-tuple-element.733, ...), kind=kOutput, calls=%fused_computation.15.clone.1 | convolution fusion | flops 547880960 | bytes 10766848 | tf_op jit(solution)/shard_map/while/body/eval_jaxpr/hgqk,khd->hgqd/dot_general | solution.py:34
  58.8 2.6 fusion.117
  62.7 2.6 bitcast_reduce_fusion.4
  65.3 4.2 %fusion.118 = f32[1,8,256,128]{3,2,1,0:T(8,128)S(1)} fusion(f32[1024,256,8]{1,0,2:T(8,128)S(1)} %get-tuple-element.732, f32[8,256]{1,0:T(8,128)S(1)} %bitcast.293, pred[1024]{0:T(1024)(128)(4,1)S(1)} %broadcast_compare_fusion.5, f32[1,8,256,128]{3,2,1,0:T(8,128)S(1)} %get-tuple-element.803, f32[8,256]{1,0:T(8,128)S(1)} %get-tuple-element.733, ...), kind=kOutput, calls=%fused_computation.15.clone.1 | convolution fusion | flops 547880960 | bytes 10766848 | tf_op jit(solution)/shard_map/while/body/eval_jaxpr/hgqk,khd->hgqd/dot_general | solution.py:34
  69.5 2.6 fusion.117
  73.4 2.6 bitcast_reduce_fusion.4
  76.0 4.2 %fusion.118 = f32[1,8,256,128]{3,2,1,0:T(8,128)S(1)} fusion(f32[1024,256,8]{1,0,2:T(8,128)S(1)} %get-tuple-element.732, f32[8,256]{1,0:T(8,128)S(1)} %bitcast.293, pred[1024]{0:T(1024)(128)(4,1)S(1)} %broadcast_compare_fusion.5, f32[1,8,256,128]{3,2,1,0:T(8,128)S(1)} %get-tuple-element.803, f32[8,256]{1,0:T(8,128)S(1)} %get-tuple-element.733, ...), kind=kOutput, calls=%fused_computation.15.clone.1 | convolution fusion | flops 547880960 | bytes 10766848 | tf_op jit(solution)/shard_map/while/body/eval_jaxpr/hgqk,khd->hgqd/dot_general | solution.py:34
  80.2 2.6 fusion.117
  84.1 2.6 bitcast_reduce_fusion.4
  86.7 4.2 %fusion.118 = f32[1,8,256,128]{3,2,1,0:T(8,128)S(1)} fusion(f32[1024,256,8]{1,0,2:T(8,128)S(1)} %get-tuple-element.732, f32[8,256]{1,0:T(8,128)S(1)} %bitcast.293, pred[1024]{0:T(1024)(128)(4,1)S(1)} %broadcast_compare_fusion.5, f32[1,8,256,128]{3,2,1,0:T(8,128)S(1)} %get-tuple-element.803, f32[8,256]{1,0:T(8,128)S(1)} %get-tuple-element.733, ...), kind=kOutput, calls=%fused_computation.15.clone.1 | convolution fusion | flops 547880960 | bytes 10766848 | tf_op jit(solution)/shard_map/while/body/eval_jaxpr/hgqk,khd->hgqd/dot_general | solution.py:34
  90.9 2.6 fusion.117
  93.5 3.0 fusion.92
  96.5 44.4 %while.50 = (s32[]{:T(128)}, f32[1,8,256]{2,1,0:T(8,128)S(1)}, f32[1,8,256]{2,1,0:T(8,128)S(1)}, f32[1,8,256,128]{3,2,1,0:T(8,128)S(1)}, s32[4]{0:T(128)S(1)}, /...) while((s32[]{:T(128)}, f32[1,8,256]{2,1,0:T(8,128)S(1)}, ...), condition=%wide.region_13.14_spmd.clone, body=%wide.region_9.13_spmd.clone.sunk | while | flops 1102416896 | bytes 29521128 | solution.py:67
  99.5 2.3 fusion.122
  101.9 3.7 %fusion.125 = f32[1,8,256,128]{3,2,1,0:T(8,128)S(1)} fusion(f32[1024,256,8]{1,0,2:T(8,128)S(1)} %get-tuple-element.749, f32[8,256]{1,0:T(8,128)S(1)} %bitcast.295, pred[256,1024]{0,1:T(8,128)(4,1)S(1)} %fusion.121, f32[1,8,256,128]{3,2,1,0:T(8,128)S(1)} %get-tuple-element.838, f32[8,256]{1,0:T(8,128)S(1)} %get-tuple-element.750, ...), kind=kOutput, calls=%fused_computation.52.clone.1 | convolution fusion | flops 547880960 | bytes 11026944 | tf_op jit(solution)/shard_map/while/body/eval_jaxpr/hgqk,khd->hgqd/dot_general | solution.py:34
  105.6 2.0 fusion.124
  110.6 2.3 fusion.122
  113.0 3.7 %fusion.125 = f32[1,8,256,128]{3,2,1,0:T(8,128)S(1)} fusion(f32[1024,256,8]{1,0,2:T(8,128)S(1)} %get-tuple-element.749, f32[8,256]{1,0:T(8,128)S(1)} %bitcast.295, pred[256,1024]{0,1:T(8,128)(4,1)S(1)} %fusion.121, f32[1,8,256,128]{3,2,1,0:T(8,128)S(1)} %get-tuple-element.838, f32[8,256]{1,0:T(8,128)S(1)} %get-tuple-element.750, ...), kind=kOutput, calls=%fused_computation.52.clone.1 | convolution fusion | flops 547880960 | bytes 11026944 | tf_op jit(solution)/shard_map/while/body/eval_jaxpr/hgqk,khd->hgqd/dot_general | solution.py:34
  116.7 2.0 fusion.124
  121.7 2.3 fusion.122
  124.1 3.7 %fusion.125 = f32[1,8,256,128]{3,2,1,0:T(8,128)S(1)} fusion(f32[1024,256,8]{1,0,2:T(8,128)S(1)} %get-tuple-element.749, f32[8,256]{1,0:T(8,128)S(1)} %bitcast.295, pred[256,1024]{0,1:T(8,128)(4,1)S(1)} %fusion.121, f32[1,8,256,128]{3,2,1,0:T(8,128)S(1)} %get-tuple-element.838, f32[8,256]{1,0:T(8,128)S(1)} %get-tuple-element.750, ...), kind=kOutput, calls=%fused_computation.52.clone.1 | convolution fusion | flops 547880960 | bytes 11026944 | tf_op jit(solution)/shard_map/while/body/eval_jaxpr/hgqk,khd->hgqd/dot_general | solution.py:34
  127.8 2.0 fusion.124
  132.8 2.3 fusion.122
  135.2 3.7 %fusion.125 = f32[1,8,256,128]{3,2,1,0:T(8,128)S(1)} fusion(f32[1024,256,8]{1,0,2:T(8,128)S(1)} %get-tuple-element.749, f32[8,256]{1,0:T(8,128)S(1)} %bitcast.295, pred[256,1024]{0,1:T(8,128)(4,1)S(1)} %fusion.121, f32[1,8,256,128]{3,2,1,0:T(8,128)S(1)} %get-tuple-element.838, f32[8,256]{1,0:T(8,128)S(1)} %get-tuple-element.750, ...), kind=kOutput, calls=%fused_computation.52.clone.1 | convolution fusion | flops 547880960 | bytes 11026944 | tf_op jit(solution)/shard_map/while/body/eval_jaxpr/hgqk,khd->hgqd/dot_general | solution.py:34
  138.9 2.0 fusion.124
  140.9 1.3 copy.43
  142.2 2.1 divide_convert_fusion
  144.4 86.7 %all-gather.5.cloned.1.call-done = bf16[4096,1024]{0,1:T(8,128)(2,1)} async-done(((bf16[256,1024]{0,1:T(8,128)(2,1)}), bf16[4096,1024]{0,1:T(8,128)(2,1)}) %all-gather.5.cloned.1.call-update) | async-done | bytes 8388624 | tf_op jit(solution)/shard_map/all_gather | solution.py:141
  231.1 9.5 %convolution_convert_fusion = bf16[4096,512]{0,1:T(8,128)(2,1)} fusion(bf16[4096,1024]{0,1:T(8,128)(2,1)} %all-gather.5.cloned.1.call-done, bf16[1024,512]{1,0:T(8,128)(2,1)S(1)} %copy-done), kind=kOutput, calls=%fused_computation.113 | convolution fusion | flops 4297064448 | bytes 13631488 | tf_op jit(solution)/shard_map/dot_general | solution.py:140
  240.7 53.6 %reduce-scatter.2.cloned.1.call-done = bf16[4096,64]{0,1:T(8,128)(2,1)} async-done(((bf16[4096,512]{0,1:T(8,128)(2,1)}), bf16[4096,64]{0,1:T(8,128)(2,1)}) %reduce-scatter.2.cloned.1.call-update) | async-done | bytes 524304 | tf_op jit(solution)/shard_map/reduce_scatter | solution.py:146
  294.3 1.1 copy.51
  295.4 18.5 %all_to_all.24 = bf16[16,256,64]{1,2,0:T(8,128)(2,1)S(1)} all-to-all(bf16[16,256,64]{1,2,0:T(8,128)(2,1)S(1)} %bitcast.299), channel_id=1, replica_groups=mesh['group'=2,'branch'=16,'tensor'=8] {'branch'}, dimensions={0} | all-to-all | bytes 1048576 | tf_op jit(solution)/shard_map/all_to_all | solution.py:149
  313.9 1.0 copy.45
  (93 shorter events, 14.9 us)
Async XLA Ops:
  6.5 224.6 %copy-start = (bf16[1024,512]{1,0:T(8,128)(2,1)S(1)}, bf16[1024,512]{1,0:T(8,128)(2,1)}, u32[]{:S(2)}) copy-start(bf16[1024,512]{1,0:T(8,128)(2,1)} %param.19) | copy-start | bytes 3145732
  6.5 15.5 %copy-start.2 = (s32[16]{0:T(128)S(1)}, s32[16]{0:T(128)}, u32[]{:S(2)}) copy-start(s32[16]{0:T(128)} %param.18) | copy-start | bytes 196
  9.3 38.2 %all-to-all-start = ((bf16[16,2,256,128]{3,2,1,0:T(8,128)(2,1)}), bf16[16,2,256,128]{3,2,1,0:T(8,128)(2,1)}, u32[]{:S(2)}, u32[]{:S(2)}) async-start(bf16[16,2,256,128]{3,2,1,0:T(8,128)(2,1)} %stack.2), calls=%async_computation | async-start | bytes 4194304 | tf_op jit(solution)/shard_map/all_to_all | solution.py:131
  17.8 75.7 %all-gather.3.cloned.1.call-start = ((), (), s32[]{:S(2)}) async-start(), calls=%async_computation.3 | async-start | bytes 2228224 | tf_op jit(solution)/shard_map/all_gather | solution.py:134
  18.5 212.6 %all-gather.5.cloned.1.call-start = ((), (), s32[]{:S(2)}) async-start(), calls=%async_computation.4 | async-start | bytes 8912896 | tf_op jit(solution)/shard_map/all_gather | solution.py:141
  26.3 4.6 %copy-start.1 = (f32[768,256,8]{1,0,2:T(8,128)S(1)}, f32[768,256,8]{1,0,2:T(8,128)}, u32[]{:S(2)}) copy-start(f32[768,256,8]{1,0,2:T(8,128)} %get-tuple-element.760) | copy-start | bytes 18874372 | tf_op jit(solution)/shard_map/while
  35.6 4.7 %copy-start.1 = (f32[768,256,8]{1,0,2:T(8,128)S(1)}, f32[768,256,8]{1,0,2:T(8,128)}, u32[]{:S(2)}) copy-start(f32[768,256,8]{1,0,2:T(8,128)} %get-tuple-element.760) | copy-start | bytes 18874372 | tf_op jit(solution)/shard_map/while
  144.4 149.9 %reduce-scatter.2.cloned.1.call-start = ((), (), s32[]{:S(2)}) async-start(), calls=%async_computation.5 | async-start | bytes 4718592 | tf_op jit(solution)/shard_map/reduce_scatter | solution.py:146
Sparse Core Ops, SparseCore 0:
  21.4 61.4 all-gather.2
  144.5 86.5 all-gather.4
  240.8 53.4 reduce-scatter.1
